TPU v7x, 128 devices: a whole 4x4x4 slice. The times are simulated.
128 devices in a mesh: grp: 4 (over x_lo, core), blk: 32 (over y, z, x_hi).
Axes of the slice: x: 4 (x_hi: 2, x_lo: 2; x = x_hi * 2 + x_lo), y: 4, z: 4, core: 2. Of those that a mesh axis runs over, the one named last changes fastest.
Arguments:
- train_grads: bfloat16 [524288, 1024], P(('grp', 'blk'))
- targets: bfloat16 [16384, 1024], P(('grp', 'blk')), may hold values from -6 to 6
Outputs:
- scores: bfloat16 [524288, 384], P(('grp', 'blk'))
All inputs are finite; a program needn't handle non-finite values.
Results may differ from a plain program's by a relative error of at most 0.014.
Values may be sent and summed in bfloat16 or wider, within the bound.
A program may use at most 128 MiB of HBM per device.

v0:
```python
import functools

import jax
import jax.numpy as jnp
from jax import lax
from jax.experimental import pallas as pl
from jax.experimental.pallas import tpu as pltpu
from jax.sharding import PartitionSpec as P

VISITS = 3
NB = 128
TILE = 256
F32 = jnp.float32
BF16 = jnp.bfloat16
MESH = pl.DeviceIdType.MESH


def panels(count):
    wide_count = count // 2
    order = [n for n in range(wide_count)]
    return [[order[-1], order[0]], order[1:-1][::-1]]


def upper_blocks(count):
    return [
        (i, c) for half in panels(count) for panel in half for c in (2 * panel, 2 * panel + 1) for i in range(c + 1)
    ]


def wide(x):
    return jnp.broadcast_to(x, (8, NB))


def split2(x):
    hi = x.astype(BF16)
    return hi, (x - hi.astype(F32)).astype(BF16)


def split3(x):
    hi = x.astype(BF16)
    rest = x - hi.astype(F32)
    mid = rest.astype(BF16)
    return hi, mid, (rest - mid.astype(F32)).astype(BF16)


def dot(a, b):
    return jnp.dot(a, b, preferred_element_type=F32)


def dot3(a, b):
    ah, al = a
    bh, bl = b
    return dot(jnp.concatenate([ah, al], axis=1), jnp.concatenate([bh, bh], axis=0)) + dot(ah, bl)


PAIRS = ((0, 0), (0, 1), (1, 0), (1, 1), (0, 2), (2, 0))


def dot6(a, b):
    left = jnp.concatenate([a[p] for p, _ in PAIRS], axis=1)
    return dot(left, jnp.concatenate([b[q] for _, q in PAIRS], axis=0))


def outer6(a, b):
    a, b = split3(a), split3(b)
    left = jnp.concatenate([a[p] for p, _ in PAIRS], axis=0)
    right = jnp.concatenate([b[q] for _, q in PAIRS], axis=0)
    return lax.dot_general(left, right, (((0,), (0,)), ((), ())), preferred_element_type=F32)


def total(terms):
    while len(terms) > 1:
        terms = [terms[i] + terms[i + 1] for i in range(0, len(terms), 2)]
    return terms[0]


def pivot_rows(rows, k, buf):
    lane = lax.broadcasted_iota(jnp.int32, (8, NB), 1)
    sub = lax.broadcasted_iota(jnp.int32, (8, NB), 0)
    y = jnp.where((lane >= k) & (lane < k + 8), -(lane == sub + k).astype(F32), rows)
    for j in range(8):
        buf[j] = wide(rows[:, k + j : k + j + 1])
    m = [buf[j] for j in range(8)]
    for b in range(0, 8, 2):
        if b == 0:
            row = lambda i, j: wide(buf[j, i : i + 1, :])
        else:
            row = lambda i, j: wide(m[j][i : i + 1, :])
        e, f, g = row(b, b), row(b, b + 1), row(b + 1, b + 1)
        inv = 1.0 / (e * g - f * f)
        ie, jf, ig = g * inv, f * inv, e * inv
        left0 = jnp.where(sub == b, -1.0, jnp.where(sub == b + 1, 0.0, m[b]))
        left1 = jnp.where(sub == b + 1, -1.0, jnp.where(sub == b, 0.0, m[b + 1]))
        pair = (sub == b) | (sub == b + 1)

        def step(x, x0, x1):
            u0, u1 = ie * x0 - jf * x1, ig * x1 - jf * x0
            return jnp.where(pair, 0.0, x) - (left0 * u0 + left1 * u1)

        for j in range(b + 2, 8):
            m[j] = step(m[j], row(b, j), row(b + 1, j))
        y = step(y, wide(y[b : b + 1, :]), wide(y[b + 1 : b + 2, :]))
    return y


def neg_inverse(a, buf, beside=()):
    lane = lax.broadcasted_iota(jnp.int32, (8, NB), 1)
    a = list(a)
    count = len(a)
    for g in range(count):
        k = 8 * g
        own = (lane >= k) & (lane < k + 8)
        rows = a[g]
        y = pivot_rows(rows, k, buf.at[g % 2])
        if g + 1 < count:
            t = a[g + 1]
            terms = [wide(t[:, k + j : k + j + 1]) * wide(y[j : j + 1, :]) for j in range(8)]
            a[g + 1] = jnp.where(own, 0.0, t) - total(terms)
        change = outer6(rows, y)
        for call in beside[g * len(beside) // count : (g + 1) * len(beside) // count]:
            call()
        for t in range(count):
            if t != g and t != g + 1:
                a[t] = jnp.where(own, 0.0, a[t]) - change[8 * t : 8 * t + 8, :]
        a[g] = y
    return a


def inverse(block, buf, beside=()):
    block = 0.5 * (block + block.T)
    tiles = [block[8 * t : 8 * t + 8, :] for t in range(NB // 8)]
    return -jnp.concatenate(neg_inverse(tiles, buf, beside), axis=0)


def solve_kernel(
    rows_total, gram_ref, right_ref, train_ref, out_ref, mat, left, right, panel, pivot, buf, held, scored, x_ref, in_sem, out_sem
):
    width = right_ref.shape[1]
    nblk = width // NB
    nrhs = right_ref.shape[0]
    rows = train_ref.shape[0]
    pieces = 8
    depth = rows // pieces
    load = pltpu.make_async_copy(train_ref, held, in_sem)
    load.start()

    eye = (lax.broadcasted_iota(jnp.int32, (NB, NB), 0) == lax.broadcasted_iota(jnp.int32, (NB, NB), 1)).astype(F32)
    blocks = upper_blocks(nblk)
    diag = jnp.zeros((NB, NB), F32)
    for n, (i, c) in enumerate(blocks):
        if i == c:
            diag = diag + gram_ref[n * NB : (n + 1) * NB, :] * eye
    trace = jnp.sum(jnp.sum(diag, axis=0, keepdims=True), axis=1, keepdims=True)
    damping = (0.1 * trace) / (rows_total * width)
    for n, (i, c) in enumerate(blocks):
        block = gram_ref[n * NB : (n + 1) * NB, :] * (1.0 / rows_total)
        if i == c:
            mat[i * NB : (i + 1) * NB, i * NB : (i + 1) * NB] = block + damping * eye
        else:
            mat[i * NB : (i + 1) * NB, c * NB : (c + 1) * NB] = block
            mat[c * NB : (c + 1) * NB, i * NB : (i + 1) * NB] = block.T
    for c in range(nrhs // NB):
        mat[:, width + c * NB : width + (c + 1) * NB] = right_ref[c * NB : (c + 1) * NB, :].astype(F32).T

    def pivot_row(j, start):
        here = pl.ds(j * NB if isinstance(j, int) else pl.multiple_of(j * NB, NB), NB)
        inv = split3(pivot[...])
        inv = jnp.concatenate([inv[p] for p, _ in PAIRS], axis=1)
        for c in range(start, width + nrhs, TILE):
            cols = slice(c, min(c + TILE, width + nrhs))
            row = split3(mat[here, cols])
            w = dot(inv, jnp.concatenate([row[q] for _, q in PAIRS], axis=0))
            wh, wl = split2(w)
            for n, part in enumerate((wh, wh, wl)):
                right[n * NB : (n + 1) * NB, cols] = part
            panel[:, cols] = w
        hi, lo = split2(mat[:, here])
        left[:, :NB] = hi
        left[:, NB : 2 * NB] = lo
        left[:, 2 * NB :] = hi
        return here

    def update(r, c):
        def call():
            some, cols = slice(r, r + TILE), slice(c, min(c + TILE, width + nrhs))
            mat[some, cols] -= dot(left[some, :], right[:, cols])

        return call

    def step(j, _):
        here = pivot_row(j, NB)
        there = pl.ds(pl.multiple_of(j * NB + NB, NB), NB)
        ahead = mat[there, there] - dot(left[there, :], right[:, there])
        calls = [update(r, c) for c in range(NB, width + nrhs, TILE) for r in range(0, width, TILE)]
        pivot[...] = inverse(ahead, buf, calls)
        mat[here, NB:] = panel[:, NB:]
        return 0

    pivot[...] = inverse(mat[:NB, :NB], buf)
    lax.fori_loop(0, nblk - 1, step, 0)
    here = pivot_row(nblk - 1, width)
    for c in range(width, width + nrhs, TILE):
        for r in range(0, width, TILE):
            update(r, c)()
    mat[here, width:] = panel[:, width:]
    x_ref[...] = mat[:, width:].astype(BF16)
    load.wait()
    scale = 1.0 / (width ** 0.5)

    def score(p, _):
        part = pl.ds(pl.multiple_of(p * depth, depth), depth)
        scored[part, :] = (dot(held[part, :], x_ref[...]) * scale).astype(BF16)
        pltpu.make_async_copy(scored.at[part], out_ref.at[part], out_sem).start()
        return 0

    lax.fori_loop(0, pieces, score, 0)
    pltpu.make_async_copy(scored, out_ref, out_sem).wait()


def solve_and_score(gram, right, train, rows_total):
    rows, width = train.shape
    nrhs = right.shape[0]
    return pl.pallas_call(
        functools.partial(solve_kernel, rows_total),
        out_shape=jax.ShapeDtypeStruct((rows, nrhs), BF16),
        in_specs=[
            pl.BlockSpec(memory_space=pltpu.VMEM),
            pl.BlockSpec(memory_space=pltpu.VMEM),
            pl.BlockSpec(memory_space=pl.ANY),
        ],
        out_specs=pl.BlockSpec(memory_space=pl.ANY),
        scratch_shapes=[
            pltpu.VMEM((width, width + nrhs), F32),
            pltpu.VMEM((width, 3 * NB), BF16),
            pltpu.VMEM((3 * NB, width + nrhs), BF16),
            pltpu.VMEM((NB, width + nrhs), F32),
            pltpu.VMEM((NB, NB), F32),
            pltpu.VMEM((2, 8, 8, NB), F32),
            pltpu.VMEM((rows, width), BF16),
            pltpu.VMEM((rows, nrhs), BF16),
            pltpu.VMEM((width, nrhs), BF16),
            pltpu.SemaphoreType.DMA,
            pltpu.SemaphoreType.DMA,
        ],
        compiler_params=pltpu.CompilerParams(vmem_limit_bytes=56 << 20),
        name="solve_and_score",
    )(gram, right, train)


RING = 4
PARTS = 3


def gram_panel(panel, known, held, turned, gram, loads, place):
    rows = held.shape[0]
    depth = rows // len(loads)
    last = (panel + 1) * 2 * NB
    for k, load in enumerate(loads):
        if load is not None:
            load.wait()
        some = slice(k * depth, (k + 1) * depth)
        if known < last:
            turned[known:last, some] = held[some, known:last].T
        res = dot(turned[:last, some], held[some, panel * 2 * NB : last])
        for n in range(2):
            c = 2 * panel + n
            for i in range(c + 1):
                spot = slice(place[i, c] * NB, place[i, c] * NB + NB)
                block = res[i * NB : (i + 1) * NB, n * NB : (n + 1) * NB]
                if k == 0:
                    gram[spot, :] = block
                else:
                    gram[spot, :] += block
    return max(known, last)


def sum_kernel(
    train_ref, target_ref, out_ref, right_ref, held, turned, gram_ref, pair, work, got1, sum1, got2, sum2, got3, full2,
    send0, recv0, send1, recv1, send2, recv2, send3, recv3, send4, recv4, send5, recv5, send6, recv6, send7, recv7,
    own_sem, load_sem,
):
    chunks = load_sem.shape[0]
    depth = held.shape[0] // chunks
    loads = [
        pltpu.make_async_copy(train_ref.at[pl.ds(k * depth, depth)], held.at[pl.ds(k * depth, depth)], load_sem.at[k])
        for k in range(chunks)
    ]
    for load in loads:
        load.start()
    nblk = held.shape[1] // NB
    halves = panels(nblk)
    place = {key: n for n, key in enumerate(upper_blocks(nblk))}
    grp, blk = lax.axis_index("grp"), lax.axis_index("blk")
    core = lax.rem(grp, 2)
    pos = (lax.rem(blk, 2) * 2 + grp // 2, blk // 8, lax.rem(blk // 2, RING))

    def device(where, which):
        x, y, z = where
        return (lax.rem(x, 2) * 2 + which, (y * RING + z) * 2 + x // 2)

    def along(axis, d):
        where = list(pos)
        where[axis] = lax.rem(where[axis] + d, RING)
        return device(where, core)

    mate = device(pos, 1 - core)
    blks = lax.axis_size("blk")
    ahead = [(grp, lax.rem(blk + s, blks)) for s in range(1, VISITS)]
    behind = [(grp, lax.rem(blk + blks - s, blks)) for s in range(1, VISITS)]
    mates = [mate] + [along(axis, d) for axis in range(3) for d in range(1, RING)]

    barrier = pltpu.get_barrier_semaphore()
    for other in mates + behind:
        pl.semaphore_signal(barrier, inc=1, device_id=other, device_id_type=MESH)

    done = [None] * chunks
    for c in range(2):

        @pl.when(core == c)
        def _():
            known = 0
            for n, panel in enumerate(halves[1 - c]):
                known = gram_panel(panel, known, held, turned, gram_ref, done if n else loads, place)

    pl.semaphore_wait(barrier, len(mates) + len(ahead))

    def remote(src, dst, send, recv, who):
        return pltpu.make_async_remote_copy(
            src_ref=src, dst_ref=dst, send_sem=send, recv_sem=recv, device_id=who, device_id_type=MESH
        )

    half = gram_ref.shape[0] // 2
    third = half // PARTS
    q1 = third // RING
    q2 = q1 // RING

    def rows(start, size):
        return pl.ds(pl.multiple_of(start, 8), size)

    c0, c1, c2, c3, c4, c5, c6, c7 = {}, {}, {}, {}, {}, {}, {}, {}
    for p in range(PARTS):
        c0[p] = remote(
            gram_ref.at[rows((1 - core) * half + p * third, third)], pair.at[p], send0.at[p], recv0.at[p], mate
        )
        c0[p].start()
    nt = target_ref.shape[0]
    for s in range(1, VISITS):
        c7[s] = remote(target_ref, right_ref.at[pl.ds(s * nt, nt)], send7.at[s - 1], recv7.at[s - 1], ahead[s - 1])
        c7[s].start()
    own = [pltpu.make_async_copy(target_ref, right_ref.at[pl.ds(0, nt)], own_sem.at[PARTS])]
    own[0].start()
    for c in range(2):

        @pl.when(core == c)
        def _():
            known = 2 * NB * (max(halves[1 - c]) + 1)
            for panel in halves[c]:
                known = gram_panel(panel, known, held, turned, gram_ref, done, place)

    steps = range(1, RING)
    for p in range(PARTS):
        axis = p
        c0[p].wait_recv()
        work[p] = gram_ref[rows(core * half + p * third, third), :] + pair[p]
        for d in steps:
            c1[p, d] = remote(
                work.at[p, rows(lax.rem(pos[axis] + d, RING) * q1, q1)],
                got1.at[p, d - 1], send1.at[p, d - 1], recv1.at[p, d - 1], along(axis, d),
            )
            c1[p, d].start()
    for p in range(PARTS):
        axis = (p + 1) % 3
        for d in steps:
            c1[p, d].wait_recv()
        mine = work[p, rows(pos[p] * q1, q1), :]
        sum1[p] = (mine + got1[p, 0]) + (got1[p, 1] + got1[p, 2])
        for d in steps:
            c2[p, d] = remote(
                sum1.at[p, rows(lax.rem(pos[axis] + d, RING) * q2, q2)],
                got2.at[p, d - 1], send2.at[p, d - 1], recv2.at[p, d - 1], along(axis, d),
            )
            c2[p, d].start()
    for p in range(PARTS):
        axis = (p + 2) % 3
        for d in steps:
            c2[p, d].wait_recv()
        mine = sum1[p, rows(pos[(p + 1) % 3] * q2, q2), :]
        sum2[p] = (mine + got2[p, 0]) + (got2[p, 1] + got2[p, 2])
        for d in steps:
            c3[p, d] = remote(sum2.at[p], got3.at[p, d - 1], send3.at[p, d - 1], recv3.at[p, d - 1], along(axis, d))
            c3[p, d].start()
    for p in range(PARTS):
        axis = (p + 1) % 3
        for d in steps:
            c3[p, d].wait_recv()
        spot = rows(pos[axis] * q2, q2)
        full2[p, spot, :] = (sum2[p] + got3[p, 0]) + (got3[p, 1] + got3[p, 2])
        for d in steps:
            c4[p, d] = remote(
                full2.at[p, spot], full2.at[p, spot], send4.at[p, d - 1], recv4.at[p, d - 1], along(axis, d)
            )
            c4[p, d].start()
    for p in range(PARTS):
        for d in steps:
            c4[p, d].wait_recv()
        spot = rows(core * half + p * third + pos[p] * q1, q1)
        for d in steps:
            c5[p, d] = remote(full2.at[p], out_ref.at[spot], send5.at[p, d - 1], recv5.at[p, d - 1], along(p, d))
            c5[p, d].start()
        c6[p, 0] = remote(full2.at[p], out_ref.at[spot], send6.at[p, 0], recv6.at[p, 0], mate)
        c6[p, 0].start()
        own.append(pltpu.make_async_copy(full2.at[p], out_ref.at[spot], own_sem.at[p]))
        own[-1].start()
    for d in (1, 3, 2):
        for p in range(PARTS):
            c5[p, d].wait_recv()
            spot = rows(core * half + p * third + lax.rem(pos[p] + RING - d, RING) * q1, q1)
            c6[p, d] = remote(out_ref.at[spot], out_ref.at[spot], send6.at[p, d], recv6.at[p, d], mate)
            c6[p, d].start()
    for copies in (c0, c1, c2, c3, c4, c5, c6, c7):
        for copy in copies.values():
            copy.wait_send()
    for copy in own:
        copy.wait()
    for copies in (c6, c7):
        for copy in copies.values():
            copy.wait_recv()


def summed_gram(train, targets):
    rows, width = train.shape
    total_rows = len(upper_blocks(width // NB)) * NB
    third = total_rows // (2 * PARTS)
    q1, q2 = third // RING, third // (RING * RING)
    sem = pltpu.SemaphoreType.DMA
    fan = RING - 1
    pairs = [(PARTS,)] + [(PARTS, fan)] * 5 + [(PARTS, RING), (VISITS - 1,)]
    return pl.pallas_call(
        sum_kernel,
        out_shape=(
            jax.ShapeDtypeStruct((total_rows, NB), F32),
            jax.ShapeDtypeStruct((VISITS * targets.shape[0], targets.shape[1]), BF16),
        ),
        in_specs=[pl.BlockSpec(memory_space=pl.ANY)] * 2,
        out_specs=[pl.BlockSpec(memory_space=pl.ANY)] * 2,
        scratch_shapes=[
            pltpu.VMEM((rows, width), BF16),
            pltpu.VMEM((width, rows), BF16),
            pltpu.VMEM((total_rows, NB), F32),
            pltpu.VMEM((PARTS, third, NB), F32),
            pltpu.VMEM((PARTS, third, NB), F32),
            pltpu.VMEM((PARTS, fan, q1, NB), F32),
            pltpu.VMEM((PARTS, q1, NB), F32),
            pltpu.VMEM((PARTS, fan, q2, NB), F32),
            pltpu.VMEM((PARTS, q2, NB), F32),
            pltpu.VMEM((PARTS, fan, q2, NB), F32),
            pltpu.VMEM((PARTS, q1, NB), F32),
        ]
        + [sem(shape) for shape in pairs for _ in range(2)]
        + [sem((PARTS + 1,)), sem((4,))],
        compiler_params=pltpu.CompilerParams(
            collective_id=0, has_side_effects=True, vmem_limit_bytes=56 << 20
        ),
        name="summed_gram",
    )(train, targets)


def per_device(train_grads, targets):
    rows_total = train_grads.shape[0] * lax.axis_size("grp") * lax.axis_size("blk")
    gram, right = summed_gram(train_grads, targets)
    return solve_and_score(gram, right, train_grads, rows_total)


def solution(mesh):
    spec = P(("grp", "blk"), None)
    return jax.shard_map(per_device, mesh=mesh, in_specs=(spec, spec), out_specs=spec, check_vma=False)
```

profile of v0, /device:TPU:1, one launch (start us, length us, event | category | flops | bytes accessed | tf_op | source)
XLA Modules:
  0.0 92.7 jit_solution(5852966295092850296)
XLA Ops:
  0.0 49.7 %summed_gram.1 = (f32[4608,128]{1,0:T(8,128)}, bf16[384,1024]{1,0:T(8,128)(2,1)}) custom-call(bf16[4096,1024]{1,0:T(8,128)(2,1)} %train_ref.3, bf16[128,1024]{1,0:T(8,128)(2,1)} %target_ref.1), custom_call_target="tpu_custom_call" | custom-call | tf_op jit(solution)/shard_map/summed_gram/pallas_call | solution.py:438
  49.7 42.8 %solve_and_score.1 = bf16[4096,384]{1,0:T(8,128)(2,1)} custom-call(f32[4608,128]{1,0:T(8,128)} %get-tuple-element.7.gram_ref, bf16[384,1024]{1,0:T(8,128)(2,1)} %get-tuple-element.8.right_ref, bf16[4096,1024]{1,0:T(8,128)(2,1)} %train_ref.3), custom_call_target="tpu_custom_call" | custom-call | tf_op jit(solution)/shard_map/solve_and_score/pallas_call | solution.py:223
where the time goes:
time: 92.8 us; the launch traced here: 92.7 us
  Pallas kernels  92.5 us (100%)
    pallas_call x1, Pallas kernels, summed_gram(): pl.pallas_call(sum_kernel, out_shape=(jax.ShapeDtypeStruct((total_rows, N...  49.7 us
    pallas_call x1, Pallas kernels, solve_and_score(): pl.pallas_call(functools.partial(solve_kernel, rows_total), out_shape=jax...  42.8 us

commit v1 on v0

--- a/solution.py
+++ b/solution.py
@@ -10,6 +10,9 @@
 VISITS = 3
 NB = 128
 TILE = 256
+NEAR = 1
+STAGES = ((0, 7),)
+ROWS = 128
 F32 = jnp.float32
 BF16 = jnp.bfloat16
 MESH = pl.DeviceIdType.MESH
@@ -112,15 +115,15 @@
         own = (lane >= k) & (lane < k + 8)
         rows = a[g]
         y = pivot_rows(rows, k, buf.at[g % 2])
-        if g + 1 < count:
-            t = a[g + 1]
-            terms = [wide(t[:, k + j : k + j + 1]) * wide(y[j : j + 1, :]) for j in range(8)]
-            a[g + 1] = jnp.where(own, 0.0, t) - total(terms)
-        change = outer6(rows, y)
+        near = range(g + 1, min(g + 1 + NEAR, count))
+        for n in near:
+            terms = [wide(a[n][:, k + j : k + j + 1]) * wide(y[j : j + 1, :]) for j in range(8)]
+            a[n] = jnp.where(own, 0.0, a[n]) - total(terms)
         for call in beside[g * len(beside) // count : (g + 1) * len(beside) // count]:
             call()
+        change = outer6(rows, y)
         for t in range(count):
-            if t != g and t != g + 1:
+            if t != g and t not in near:
                 a[t] = jnp.where(own, 0.0, a[t]) - change[8 * t : 8 * t + 8, :]
         a[g] = y
     return a
@@ -162,11 +165,11 @@
     for c in range(nrhs // NB):
         mat[:, width + c * NB : width + (c + 1) * NB] = right_ref[c * NB : (c + 1) * NB, :].astype(F32).T
 
-    def pivot_row(j, start):
-        here = pl.ds(j * NB if isinstance(j, int) else pl.multiple_of(j * NB, NB), NB)
-        inv = split3(pivot[...])
-        inv = jnp.concatenate([inv[p] for p, _ in PAIRS], axis=1)
-        for c in range(start, width + nrhs, TILE):
+    def rows_of(j):
+        return pl.ds(j * NB if isinstance(j, int) else pl.multiple_of(j * NB, NB), NB)
+
+    def pivot_row(here, inv, c):
+        def call():
             cols = slice(c, min(c + TILE, width + nrhs))
             row = split3(mat[here, cols])
             w = dot(inv, jnp.concatenate([row[q] for _, q in PAIRS], axis=0))
@@ -174,33 +177,52 @@
             for n, part in enumerate((wh, wh, wl)):
                 right[n * NB : (n + 1) * NB, cols] = part
             panel[:, cols] = w
-        hi, lo = split2(mat[:, here])
-        left[:, :NB] = hi
-        left[:, NB : 2 * NB] = lo
-        left[:, 2 * NB :] = hi
-        return here
+
+        return call
+
+    def pivot_column(here, some):
+        hi, lo = split2(mat[some, here])
+        left[some, :NB] = hi
+        left[some, NB : 2 * NB] = lo
+        left[some, 2 * NB :] = hi
 
     def update(r, c):
         def call():
-            some, cols = slice(r, r + TILE), slice(c, min(c + TILE, width + nrhs))
+            some, cols = slice(r, r + ROWS), slice(c, min(c + TILE, width + nrhs))
             mat[some, cols] -= dot(left[some, :], right[:, cols])
 
         return call
 
-    def step(j, _):
-        here = pivot_row(j, NB)
-        there = pl.ds(pl.multiple_of(j * NB + NB, NB), NB)
-        ahead = mat[there, there] - dot(left[there, :], right[:, there])
-        calls = [update(r, c) for c in range(NB, width + nrhs, TILE) for r in range(0, width, TILE)]
+    def stacked_inverse():
+        inv = split3(pivot[...])
+        return jnp.concatenate([inv[p] for p, _ in PAIRS], axis=1)
+
+    def step(start, j, _):
+        here, there = rows_of(j), rows_of(j + 1)
+        inv = stacked_inverse()
+        w = dot(inv, jnp.concatenate([split3(mat[here, there])[q] for _, q in PAIRS], axis=0))
+        wh, wl = split2(w)
+        hi, lo = split2(mat[there, here])
+        ahead = mat[there, there] - dot(
+            jnp.concatenate([hi, lo, hi], axis=1), jnp.concatenate([wh, wh, wl], axis=0)
+        )
+        pivot_column(here, slice(0, width))
+        calls = []
+        for c in range(start, width + nrhs, TILE):
+            pivot_row(here, inv, c)()
+            calls += [update(r, c) for r in range(0, width, ROWS)]
         pivot[...] = inverse(ahead, buf, calls)
-        mat[here, NB:] = panel[:, NB:]
+        mat[here, start:] = panel[:, start:]
         return 0
 
     pivot[...] = inverse(mat[:NB, :NB], buf)
-    lax.fori_loop(0, nblk - 1, step, 0)
-    here = pivot_row(nblk - 1, width)
+    for first, last in STAGES:
+        lax.fori_loop(first, last, functools.partial(step, (first + 1) * NB), 0)
+    here = rows_of(nblk - 1)
+    pivot_column(here, slice(0, width))
     for c in range(width, width + nrhs, TILE):
-        for r in range(0, width, TILE):
+        pivot_row(here, stacked_inverse(), c)()
+        for r in range(0, width, ROWS):
             update(r, c)()
     mat[here, width:] = panel[:, width:]
     x_ref[...] = mat[:, width:].astype(BF16)

time: 92.8 us -> 88.8 us (0.957)
  Pallas kernels: 92.5 us -> 88.6 us
    pallas_call x1, Pallas kernels: 42.8 us -> 38.9 us  [solve_and_score(): pl.pallas_call(functools.partial(solve_kernel, rows_total), out_shape=jax...]
where the time goes in v1:
time: 88.8 us; the launch traced here: 88.7 us
  Pallas kernels  88.6 us (100%)
    pallas_call x1, Pallas kernels, summed_gram(): pl.pallas_call(sum_kernel, out_shape=(jax.ShapeDtypeStruct((total_rows, N...  49.7 us
    pallas_call x1, Pallas kernels, solve_and_score(): pl.pallas_call(functools.partial(solve_kernel, rows_total), out_shape=jax...  38.9 us

profile of v1, /device:TPU:1, one launch (start us, length us, event | category | flops | bytes accessed | tf_op | source)
XLA Modules:
  0.0 88.7 jit_solution(9179919283015915645)
XLA Ops:
  0.0 49.7 %summed_gram.1 = (f32[4608,128]{1,0:T(8,128)}, bf16[384,1024]{1,0:T(8,128)(2,1)}) custom-call(bf16[4096,1024]{1,0:T(8,128)(2,1)} %train_ref.3, bf16[128,1024]{1,0:T(8,128)(2,1)} %target_ref.1), custom_call_target="tpu_custom_call" | custom-call | tf_op jit(solution)/shard_map/summed_gram/pallas_call | solution.py:460
  49.7 38.9 %solve_and_score.1 = bf16[4096,384]{1,0:T(8,128)(2,1)} custom-call(f32[4608,128]{1,0:T(8,128)} %get-tuple-element.7.gram_ref, bf16[384,1024]{1,0:T(8,128)(2,1)} %get-tuple-element.8.right_ref, bf16[4096,1024]{1,0:T(8,128)(2,1)} %train_ref.3), custom_call_target="tpu_custom_call" | custom-call | tf_op jit(solution)/shard_map/solve_and_score/pallas_call | solution.py:245

commit v2 on v1

--- a/solution.py
+++ b/solution.py
@@ -142,7 +142,7 @@
     nblk = width // NB
     nrhs = right_ref.shape[0]
     rows = train_ref.shape[0]
-    pieces = 8
+    pieces = 2
     depth = rows // pieces
     load = pltpu.make_async_copy(train_ref, held, in_sem)
     load.start()
@@ -155,15 +155,26 @@
             diag = diag + gram_ref[n * NB : (n + 1) * NB, :] * eye
     trace = jnp.sum(jnp.sum(diag, axis=0, keepdims=True), axis=1, keepdims=True)
     damping = (0.1 * trace) / (rows_total * width)
-    for n, (i, c) in enumerate(blocks):
-        block = gram_ref[n * NB : (n + 1) * NB, :] * (1.0 / rows_total)
-        if i == c:
-            mat[i * NB : (i + 1) * NB, i * NB : (i + 1) * NB] = block + damping * eye
-        else:
-            mat[i * NB : (i + 1) * NB, c * NB : (c + 1) * NB] = block
-            mat[c * NB : (c + 1) * NB, i * NB : (i + 1) * NB] = block.T
-    for c in range(nrhs // NB):
-        mat[:, width + c * NB : width + (c + 1) * NB] = right_ref[c * NB : (c + 1) * NB, :].astype(F32).T
+    first = gram_ref[blocks.index((0, 0)) * NB : (blocks.index((0, 0)) + 1) * NB, :] * (1.0 / rows_total) + damping * eye
+
+    def fill(n, i, c):
+        def call():
+            block = gram_ref[n * NB : (n + 1) * NB, :] * (1.0 / rows_total)
+            if i == c:
+                mat[i * NB : (i + 1) * NB, i * NB : (i + 1) * NB] = block + damping * eye
+            else:
+                mat[i * NB : (i + 1) * NB, c * NB : (c + 1) * NB] = block
+                mat[c * NB : (c + 1) * NB, i * NB : (i + 1) * NB] = block.T
+
+        return call
+
+    def fill_right(c):
+        def call():
+            mat[:, width + c * NB : width + (c + 1) * NB] = right_ref[c * NB : (c + 1) * NB, :].astype(F32).T
+
+        return call
+
+    fills = [fill(n, i, c) for n, (i, c) in enumerate(blocks)] + [fill_right(c) for c in range(nrhs // NB)]
 
     def rows_of(j):
         return pl.ds(j * NB if isinstance(j, int) else pl.multiple_of(j * NB, NB), NB)
@@ -215,7 +226,7 @@
         mat[here, start:] = panel[:, start:]
         return 0
 
-    pivot[...] = inverse(mat[:NB, :NB], buf)
+    pivot[...] = inverse(first, buf, fills)
     for first, last in STAGES:
         lax.fori_loop(first, last, functools.partial(step, (first + 1) * NB), 0)
     here = rows_of(nblk - 1)

time: 88.8 us -> 88.2 us (level)
  no operation moved by 1% of the time
where the time goes in v2:
time: 88.2 us; the launch traced here: 88.1 us
  Pallas kernels  88 us (100%)
    pallas_call x1, Pallas kernels, summed_gram(): pl.pallas_call(sum_kernel, out_shape=(jax.ShapeDtypeStruct((total_rows, N...  49.7 us
    pallas_call x1, Pallas kernels, solve_and_score(): pl.pallas_call(functools.partial(solve_kernel, rows_total), out_shape=jax...  38.3 us

profile of v2, /device:TPU:1, one launch (start us, length us, event | category | flops | bytes accessed | tf_op | source)
XLA Modules:
  0.0 88.1 jit_solution(17072021583935095903)
XLA Ops:
  0.0 49.7 %summed_gram.1 = (f32[4608,128]{1,0:T(8,128)}, bf16[384,1024]{1,0:T(8,128)(2,1)}) custom-call(bf16[4096,1024]{1,0:T(8,128)(2,1)} %train_ref.3, bf16[128,1024]{1,0:T(8,128)(2,1)} %target_ref.1), custom_call_target="tpu_custom_call" | custom-call | tf_op jit(solution)/shard_map/summed_gram/pallas_call | solution.py:471
  49.7 38.3 %solve_and_score.1 = bf16[4096,384]{1,0:T(8,128)(2,1)} custom-call(f32[4608,128]{1,0:T(8,128)} %get-tuple-element.7.gram_ref, bf16[384,1024]{1,0:T(8,128)(2,1)} %get-tuple-element.8.right_ref, bf16[4096,1024]{1,0:T(8,128)(2,1)} %train_ref.3), custom_call_target="tpu_custom_call" | custom-call | tf_op jit(solution)/shard_map/solve_and_score/pallas_call | solution.py:256
